TPU v7x, 32 devices: a whole 2x2x4 slice. The times are simulated.
32 devices in a mesh: harm: 4 (over y, x), node: 8 (over z, core).
Axes of the slice: x: 2, y: 2, z: 4, core: 2. Of those that a mesh axis runs over, the one named last changes fastest.
Arguments:
- voltages: float32 [128, 8192], P('harm', 'node'), may hold values from -6 to 6
- conductance: float32 [64, 3, 128, 128], P('node'), may hold values from -0.3125 to 0.3125
- capacitance: float32 [64, 3, 128, 128], P('node'), may hold values from -0.3125 to 0.3125
- pattern: int32 [64, 3], P('node'), may hold values from 0 to 63, as said below
- samples: float32 [256, 8192], P(None, 'node'), may hold values from 0.1 to 2
- terminals: int32 [2, 8192], P(None, 'node'), may hold values from 0 to 8191, as said below
Outputs:
- product: float32 [128, 8192], P('harm', 'node')
Inputs may be any that keep to these rules, and one draw needn't show every extreme that they name: `pattern`: slot 0 of row block r is r itself; every slot names a block within one block of the 8 row blocks of the device that holds r; the first row block of every device but the first names the block just before that range in slot 1, the last row block of every device but the last names the block just after it in slot 2. `terminals`: branch m belongs to the device holding nodes from 1024 * (m // 1024) on; its first terminal lies among that device's 1024 nodes, its second among those or the 128 nodes after them.
All inputs are finite; a program needn't handle non-finite values.
Results may differ from a plain program's by a relative error of at most 0.0003.
Values sent between devices are 32-bit elements; how exact they have to be, the bound alone decides.
A program may use at most 64 MiB of HBM per device.

v0:
```python
import math

import jax
import jax.numpy as jnp
from jax import lax
from jax.sharding import PartitionSpec as P

highest = lax.Precision.HIGHEST


def with_halo(block, sides, width):
    for axis, dim in sides:
        count = lax.axis_size(axis)
        forward = [(i, i + 1) for i in range(count - 1)]
        backward = [(target, source) for source, target in forward]
        low = lax.ppermute(
            lax.slice_in_dim(block, block.shape[dim] - width, None, axis=dim), axis, forward
        )
        high = lax.ppermute(lax.slice_in_dim(block, 0, width, axis=dim), axis, backward)
        block = jnp.concatenate([low, block, high], axis=dim)
    return block


def from_behind(value, axis, by):
    devices = lax.axis_size(axis)
    pairs = [(i, i + by) for i in range(devices) if 0 <= i + by < devices]
    return lax.ppermute(value, axis, pairs)


def rotate_pairs(field, angular):
    column_count, width_now = field.shape
    paired = field.reshape(column_count // 2, 2, width_now)
    turned = jnp.stack([-paired[:, 1], paired[:, 0]], axis=1) * angular[:, None, None]
    return turned.reshape(column_count, width_now)


def per_device(voltages, conductance, capacitance, pattern, samples, terminals):
    local_count, node_count = voltages.shape
    block_size = conductance.shape[2]
    block_count = node_count // block_size
    harm_devices = lax.axis_size("harm")
    harm_index = lax.axis_index("harm")
    node_index = lax.axis_index("node")
    harm_local = local_count // 2
    total_harm = harm_local * harm_devices
    branch_count = samples.shape[1]
    period = samples.shape[0]
    padded = with_halo(voltages, (("node", 1),), block_size)
    padded_tiles = padded.reshape(local_count, block_count + 2, block_size)
    local_pattern = pattern - (node_index * block_count - 1)
    picked = jnp.take(padded_tiles, local_pattern, axis=1)
    conductive = jnp.einsum("crjk,rjkl->crl", picked, conductance, precision=highest).reshape(
        local_count, node_count
    )
    capacitive = jnp.einsum("crjk,rjkl->crl", picked, capacitance, precision=highest).reshape(
        local_count, node_count
    )
    harm_order = harm_index * harm_local + jnp.arange(harm_local, dtype=jnp.int32)
    angular = harm_order.astype(jnp.float32) / total_harm
    linear = conductive + rotate_pairs(capacitive, angular)
    offset = node_index * node_count - block_size
    first_end = terminals[0] - offset
    second_end = terminals[1] - offset
    span = harm_local + 2 * total_harm - 2
    frequency = harm_index * harm_local - (total_harm - 1) + jnp.arange(span, dtype=jnp.int32)
    sample_index = jnp.arange(period, dtype=jnp.int32)
    phases = jnp.mod(frequency[:, None] * sample_index[None, :], period)
    angles = phases.astype(jnp.float32) * (2.0 * math.pi / period)
    spectral_table = jnp.concatenate([jnp.cos(angles), -jnp.sin(angles)], axis=0) / period
    spectrum = jnp.dot(spectral_table, samples, precision=highest).reshape(2, span, branch_count)
    own_harm = jnp.arange(harm_local, dtype=jnp.int32)
    piece = lax.all_gather(padded, "harm", axis=0, tiled=True)
    piece_harm = piece.shape[0] // 2
    branch = jnp.take(piece, first_end, axis=1) - jnp.take(piece, second_end, axis=1)
    paired = branch.reshape(piece_harm, 2, branch_count)
    other_harm = jnp.arange(piece_harm, dtype=jnp.int32)
    diff_index = own_harm[:, None] - other_harm[None, :] + total_harm - 1
    sum_index = own_harm[:, None] + other_harm[None, :] + total_harm - 1
    diff_coef = jnp.take(spectrum, diff_index, axis=1)
    sum_coef = jnp.take(spectrum, sum_index, axis=1)
    real_in = paired[None, :, 0]
    imag_in = paired[None, :, 1]
    real_out = jnp.sum(
        (diff_coef[0] + sum_coef[0]) * real_in + (sum_coef[1] - diff_coef[1]) * imag_in, axis=1
    )
    imag_out = jnp.sum(
        (diff_coef[0] - sum_coef[0]) * imag_in + (diff_coef[1] + sum_coef[1]) * real_in, axis=1
    )
    folded = jnp.stack([real_out, imag_out], axis=1)
    current = folded.reshape(local_count, branch_count)
    injected = jnp.zeros((local_count, node_count + 2 * block_size), jnp.float32)
    injected = injected.at[:, first_end].add(current).at[:, second_end].add(-current)
    spilled = from_behind(injected[:, node_count + block_size :], "node", 1)
    owned = injected[:, block_size : node_count + block_size]
    arrival = jnp.concatenate(
        [spilled, jnp.zeros((local_count, node_count - block_size), jnp.float32)], axis=1
    )
    return linear + owned + arrival


def solution(mesh):
    in_specs = (
        P("harm", "node"),
        P("node", None, None, None),
        P("node", None, None, None),
        P("node", None),
        P(None, "node"),
        P(None, "node"),
    )
    out_specs = P("harm", "node")
    return jax.shard_map(
        per_device, mesh=mesh, in_specs=in_specs, out_specs=out_specs, check_vma=False
    )
```

profile of v0, /device:TPU:0, one launch (start us, length us, event | category | flops | bytes accessed | tf_op | source)
XLA Modules:
  0.0 136.0 jit_solution(10504396634800899863)
XLA Ops:
  0.0 0.9 fusion.35
  0.9 2.3 %collective-permute-start = (f32[32,128]{1,0:T(8,128)S(1)}, f32[32,128]{1,0:T(8,128)S(1)}, u32[]{:S(2)}, u32[]{:S(2)}) collective-permute-start(f32[32,128]{1,0:T(8,128)S(1)} %get-tuple-element.23), channel_id=1, source_target_pairs={{0,1},{1,2},{2,3},{3,4},{4,5},{5,6},{6,7},{8,9},{9,10},{10,11},{11... | collective-permute-start | bytes 49160 | tf_op jit(solution)/shard_map/ppermute | solution.py:16
  3.2 1.3 collective-permute-start.1
  4.6 0.8 compare_select_fusion
  5.4 0.7 fusion.27
  6.1 2.4 %fusion.11 = f32[284,1024]{1,0:T(8,128)S(1)} fusion(f32[256,1024]{1,0:T(8,128)} %param.14, f32[142,256]{1,0:T(8,128)S(1)} %get-tuple-element.27, f32[142,256]{1,0:T(8,128)S(1)} %get-tuple-element.26), kind=kOutput, calls=%fused_computation.30 | convolution fusion | flops 893532160 | bytes 2502656 | tf_op jit(solution)/shard_map/dot_general | solution.py:70
  8.5 1.1 reshape.97
  9.6 2.2 %copy.82 = f32[2,142,1024]{2,0,1:T(2,128)S(1)} copy(f32[2,142,1024]{2,1,0:T(8,128)} %reshape.97) | data formatting | bytes 2326528 | tf_op jit(solution)/shard_map/reshape | solution.py:70
  11.8 0.1 copy.78
  11.9 0.1 reshape.134
  12.0 0.1 reshape.168
  12.0 17.2 %gather_fusion.2 = f32[1024,2,1024]{2,1,0:T(2,128)} fusion(f32[2,142,1024]{2,0,1:T(2,128)S(1)} %copy.82, s32[1024]{0:T(1024)S(1)} %get-tuple-element.29), kind=kCustom, calls=%fused_computation.2.clone | custom fusion | bytes 16781312 | tf_op jit(solution)/shard_map/jit(_take)/gather | solution.py:80
  29.3 6.7 %fusion = f32[2,16,64,1024]{3,2,1,0:T(8,128)S(1)} fusion(f32[16,64,2,1024]{3,2,1,0:T(2,128)} %bitcast.81, pred[16,64]{1,0:T(8,128)(4,1)S(1)} %compare_and_fusion), kind=kLoop, calls=%fused_computation.8 | loop fusion | flops 2097152 | bytes 16778240 | tf_op jit(solution)/shard_map/jit(_take)/select_n | solution.py:80
  36.0 3.2 %copy-done.1 = f32[2,16,64,1024]{3,2,1,0:T(8,128)} copy-done((f32[2,16,64,1024]{3,2,1,0:T(8,128)}, f32[2,16,64,1024]{3,2,1,0:T(8,128)S(1)}, u32[]{:S(2)}) %copy-start.1) | copy-done | bytes 8388632
  39.2 2.2 %slice.75 = f32[1,16,64,1024]{3,2,1,0:T(8,128)} slice(f32[2,16,64,1024]{3,2,1,0:T(8,128)S(1)} %fusion), slice={[1:2], [0:16], [0:64], [0:1024]} | slice | bytes 8388608 | tf_op jit(solution)/shard_map/slice | solution.py:84
  41.5 0.1 reshape.164
  41.6 17.3 %gather_fusion.1 = f32[1024,2,1024]{2,1,0:T(2,128)} fusion(f32[2,142,1024]{2,0,1:T(2,128)S(1)} %copy.82, s32[1024]{0:T(1024)S(1)} %broadcast_clamp_fusion.1), kind=kCustom, calls=%fused_computation.clone | custom fusion | bytes 16781312 | tf_op jit(solution)/shard_map/jit(_take)/gather | solution.py:79
  58.9 6.4 %select_bitcast_fusion = f32[2,16,64,1024]{3,0,2,1:T(2,128)S(1)} fusion(f32[16,64,2,1024]{3,2,1,0:T(2,128)} %bitcast.80, pred[16,64]{1,0:T(8,128)(4,1)S(1)} %compare_and_fusion.1), kind=kLoop, calls=%fused_computation.9 | loop fusion | flops 2097152 | bytes 16778240 | tf_op jit(solution)/shard_map/jit(_take)/select_n | solution.py:79
  65.3 15.4 %copy_add_fusion = (f32[1,16,64,1024]{3,0,2,1:T(1,128)}, f32[1,16,64,1024]{3,0,2,1:T(1,128)}, f32[1,16,64,1024]{3,0,2,1:T(1,128)}) fusion(f32[1,16,64,1024]{3,2,1,0:T(8,128)S(1)} %copy-done.2, f32[2,16,64,1024]{3,0,2,1:T(2,128)S(1)} %select_bitcast_fusion), kind=kLoop, calls=%fused_computation.18 | loop fusion | flops 1048576 | bytes 25165824 | tf_op jit(solution)/shard_map/add | solution.py:87
  80.6 0.1 copy.77
  80.7 0.1 mul.76
  80.8 0.1 mul.77
  81.0 12.7 %all_gather.3 = f32[128,1280]{1,0:T(8,128)S(1)} all-gather(f32[32,1280]{1,0:T(8,128)S(1)} %constant_dynamic-update-slice_fusion), channel_id=1, replica_groups=mesh['harm'=4,'node'=8] {'harm'}, dimensions={0}, use_global_device_ids=true | all-gather | bytes 819200 | tf_op jit(solution)/shard_map/all_gather | solution.py:72
  93.7 0.2 copy.86
  94.0 2.8 %gather_fusion.4 = f32[1024,128]{1,0:T(8,128)S(1)} fusion(f32[128,1280]{0,1:T(8,128)S(1)} %copy.86, s32[1024]{0:T(1024)S(1)} %get-tuple-element.31), kind=kCustom, calls=%fused_computation.3.clone | custom fusion | bytes 1052672 | tf_op jit(solution)/shard_map/jit(_take)/gather | solution.py:74
  96.8 4.0 %gather_fusion.3 = f32[1024,128]{1,0:T(8,128)} fusion(f32[128,1280]{0,1:T(8,128)S(1)} %copy.86, s32[1024]{0:T(1024)S(1)} %get-tuple-element.30), kind=kCustom, calls=%fused_computation.1.clone | custom fusion | bytes 1052672 | tf_op jit(solution)/shard_map/jit(_take)/gather | solution.py:74
  100.8 1.4 %bitcast_subtract_fusion = f32[128,1024]{0,1:T(8,128)S(1)} fusion(f32[1024,128]{1,0:T(8,128)S(1)} %gather_fusion.4, f32[1024,128]{1,0:T(8,128)} %gather_fusion.3, pred[1024]{0:T(1024)(128)(4,1)S(1)} %get-tuple-element.32, pred[1024]{0:T(1024)(128)(4,1)S(1)} %get-tuple-element.33), kind=kLoop, calls=%fused_computation.22 | loop fusion | flops 393216 | bytes 1574912 | tf_op jit(solution)/shard_map/sub | solution.py:74
  102.1 0.2 copy.88
  102.4 0.3 reshape.98
  102.7 0.4 fusion.34
  103.2 10.1 %fusion.4 = (f32[16,1024]{1,0:T(8,128)S(1)}, f32[16,1024]{1,0:T(8,128)S(1)}) fusion(f32[1,16,64,1024]{3,0,2,1:T(1,128)} %get-tuple-element.16, f32[2,16,64,1024]{3,2,1,0:T(8,128)} %copy-done.1, f32[1,16,64,1024]{3,0,2,1:T(1,128)} %get-tuple-element.17, f32[64,1024]{1,0:T(8,128)S(1)} %bitcast.85, f32[64,1024]{1,0:T(8,128)S(1)} %bitcast.86, ...), kind=kLoop, calls=%fused_computation.16 | loop fusion | flops 11501568 | bytes 21626880 | tf_op jit(solution)/shard_map/reduce_sum | solution.py:83
  113.3 0.1 copy.91
  113.4 0.1 reshape.141
  113.5 1.0 copy.92
  114.5 0.2 copy.93
  114.7 6.6 %scatter_custom_fusion = f32[32,1280]{0,1:T(8,128)S(1)} fusion(s32[1024]{0:T(1024)S(1)} %bitcast.94, f32[1024,32]{1,0:T(8,128)} %copy.92, f32[]{:T(128)} %constant.85.clone.1), kind=kCustom, calls=%fused_computation.27 | custom fusion | flops 32768 | bytes 164352 | tf_op jit(solution)/shard_map/scatter-add | solution.py:92
  121.3 6.3 %scatter_fusion = f32[32,1280]{0,1:T(8,128)S(1)} fusion(f32[32,1280]{0,1:T(8,128)S(1)} %scatter_custom_fusion, s32[1024]{0:T(1024)S(1)} %bitcast.93, f32[1024,32]{1,0:T(8,128)S(1)} %copy.93), kind=kCustom, calls=%fused_computation.6 | custom fusion | flops 32768 | bytes 397312 | tf_op jit(solution)/shard_map/scatter-add | solution.py:92
  127.7 2.6 %collective-permute-start.2 = (f32[32,128]{1,0:T(8,128)S(1)}, f32[32,128]{1,0:T(8,128)S(1)}, u32[]{:S(2)}, u32[]{:S(2)}) collective-permute-start(f32[32,128]{1,0:T(8,128)S(1)} %copy.103), channel_id=1, source_target_pairs={{0,1},{1,2},{2,3},{3,4},{4,5},{5,6},{6,7},{8,9},{9,10},{10,11},{11... | collective-permute-start | bytes 49160 | tf_op jit(solution)/shard_map/ppermute | solution.py:27
  130.2 0.6 gather_fusion
  130.8 1.1 convolution_bitcast_fusion.1
  132.0 2.5 %convolution_bitcast_fusion = f32[32,8,128]{2,0,1:T(8,128)S(1)} fusion(f32[8,3,128,128]{3,2,1,0:T(8,128)} %param.12, f32[8,3,32,128]{3,2,1,0:T(8,128)S(1)} %bitcast.83, pred[8,3]{1,0:T(8,128)(4,1)S(1)} %copy.77), kind=kOutput, calls=%fused_computation.20 | convolution fusion | flops 151093248 | bytes 2097176 | tf_op jit(solution)/shard_map/crjk,rjkl->crl/dot_general | solution.py:55
  134.5 0.1 copy.81
  134.6 0.1 reshape_reshape.3
  134.7 0.1 slice_negate_fusion
  134.8 0.1 pad_maximum_fusion
  135.0 0.2 copy.102
  135.2 0.1 stack.16
  135.3 0.7 fusion.26
  (34 shorter events, 0.4 us)
Async XLA Ops:
  0.0 130.8 %copy-start = (f32[8,3,128,128]{3,2,1,0:T(8,128)S(1)}, f32[8,3,128,128]{3,2,1,0:T(8,128)}, u32[]{:S(2)}) copy-start(f32[8,3,128,128]{3,2,1,0:T(8,128)} %param.11) | copy-start | bytes 4718596
  0.0 11.8 %copy-start.4 = (s32[8,3]{0,1:T(4,128)S(1)}, s32[8,3]{0,1:T(4,128)}, u32[]{:S(2)}) copy-start(s32[8,3]{0,1:T(4,128)} %param.13) | copy-start | bytes 292
  0.9 80.0 %collective-permute-start = (f32[32,128]{1,0:T(8,128)S(1)}, f32[32,128]{1,0:T(8,128)S(1)}, u32[]{:S(2)}, u32[]{:S(2)}) collective-permute-start(f32[32,128]{1,0:T(8,128)S(1)} %get-tuple-element.23), channel_id=1, source_target_pairs={{0,1},{1,2},{2,3},{3,4},{4,5},{5,6},{6,7},{8,9},{9,10},{10,11},{11... | collective-permute-start | bytes 49160 | tf_op jit(solution)/shard_map/ppermute | solution.py:16
  3.2 77.7 %collective-permute-start.1 = (f32[32,128]{1,0:T(8,128)S(1)}, f32[32,128]{1,0:T(8,128)S(1)}, u32[]{:S(2)}, u32[]{:S(2)}) collective-permute-start(f32[32,128]{1,0:T(8,128)S(1)} %get-tuple-element.22), channel_id=1, source_target_pairs={{1,0},{2,1},{3,2},{4,3},{5,4},{6,5},{7,6},{9,8},{10,9},{11,10},{12... | collective-permute-start | bytes 49160 | tf_op jit(solution)/shard_map/ppermute | solution.py:19
  36.0 3.2 %copy-start.1 = (f32[2,16,64,1024]{3,2,1,0:T(8,128)}, f32[2,16,64,1024]{3,2,1,0:T(8,128)S(1)}, u32[]{:S(2)}) copy-start(f32[2,16,64,1024]{3,2,1,0:T(8,128)S(1)} %fusion) | copy-start | bytes 25165828
  58.9 6.4 %copy-start.2 = (f32[1,16,64,1024]{3,2,1,0:T(8,128)S(1)}, f32[1,16,64,1024]{3,2,1,0:T(8,128)}, u32[]{:S(2)}) copy-start(f32[1,16,64,1024]{3,2,1,0:T(8,128)} %slice.75) | copy-start | bytes 12582916
  65.3 15.7 %copy-start.3 = (f32[32,1024]{1,0:T(8,128)S(1)}, f32[32,1024]{1,0:T(8,128)}, u32[]{:S(2)}) copy-start(f32[32,1024]{1,0:T(8,128)} %param.10) | copy-start | bytes 393220
  127.7 7.6 %collective-permute-start.2 = (f32[32,128]{1,0:T(8,128)S(1)}, f32[32,128]{1,0:T(8,128)S(1)}, u32[]{:S(2)}, u32[]{:S(2)}) collective-permute-start(f32[32,128]{1,0:T(8,128)S(1)} %copy.103), channel_id=1, source_target_pairs={{0,1},{1,2},{2,3},{3,4},{4,5},{5,6},{6,7},{8,9},{9,10},{10,11},{11... | collective-permute-start | bytes 49160 | tf_op jit(solution)/shard_map/ppermute | solution.py:27
where the time goes:
time: 139 us; the launch traced here: 136 us
  local copies, waits for them, and re-layouts  55.3 us (40%)
  other arithmetic  55.3 us (40%)
  blocking collectives  12.7 us (9%)
  starting transfers between devices  6.2 us (4%)
  matrix products  6.04 us (4%)
    gather x1, local copies, waits for them, and re-layouts, per_device(): diff_coef = jnp.take(spectrum, diff_index, axis=1)  17.3 us
    gather x1, local copies, waits for them, and re-layouts, per_device(): sum_coef = jnp.take(spectrum, sum_index, axis=1)  17.2 us
    add x1, other arithmetic, per_device(): diff_coef[1] + sum_coef[1]  15.4 us
    scatter-add x2, other arithmetic, per_device(): injected.at[:, first_end].add(current).at[:, second_end].add(-current)  12.9 us
    all_gather x1, blocking collectives, per_device(): piece = lax.all_gather(padded, 'harm', axis=0, tiled=True)  12.7 us
    reduce_sum x1, other arithmetic, per_device(): jnp.sum((diff_coef[0] + sum_coef[0]) * real_in + (sum_coef[1] - diff_coef...  10.1 us
    select_n x2, other arithmetic, per_device(): sum_coef = jnp.take(spectrum, sum_index, axis=1)  6.7 us
    select_n x2, other arithmetic, per_device(): diff_coef = jnp.take(spectrum, diff_index, axis=1)  6.39 us
  transfers between devices with their start and end apart: 3, of which 0 were waited for; matrix products, arithmetic and copies ran while one was open for 57% of the time, Pallas kernels for 0%

commit v1 on v0

v1 whole, which is shorter than its diff:
```python
import functools
import math

import jax
import jax.numpy as jnp
import ml_dtypes
import numpy as np
from jax import lax
from jax.experimental import pallas as pl
from jax.experimental.pallas import tpu as pltpu
from jax.sharding import PartitionSpec as P

MESH = pl.DeviceIdType.MESH
f32, bf16 = jnp.float32, jnp.bfloat16


def halves(value):
    high = value.astype(bf16).astype(f32)
    return jnp.concatenate([high, value - high], axis=0).astype(bf16)


def dot(a, b):
    return jnp.dot(a, b, preferred_element_type=f32)


def dot_t(a, b):
    return lax.dot_general(a, b, (((1,), (1,)), ((), ())), preferred_element_type=f32)


def kernel(
    H, N, parts, dup,
    pat, term, v_in, g_in, c_in, s_in, f_in, b_in,
    out,
    v_vm, g_vm, c_vm, s_vm, f_vm, b_vm,
    vext, halo, ends, send_b, recv_b, send_c, recv_c, send_s, recv_s, lin,
    load_sem, gc_sem,
    low_send, low_recv, halo_send, halo_recv,
    b_send, b_recv, c_send, c_recv, s_send, s_recv,
):
    h, n = lax.axis_index("harm"), lax.axis_index("node")
    rows, nodes = v_vm.shape
    blocks, slots, blk, _ = g_vm.shape
    chunk = s_vm.shape[1]
    part, twin = h // dup, lax.rem(h, dup)
    offset = pl.multiple_of(part * chunk, 128)

    load_v = pltpu.make_async_copy(v_in, v_vm, load_sem.at[0])
    load_f = pltpu.make_async_copy(f_in, f_vm, load_sem.at[1])
    load_b = pltpu.make_async_copy(b_in, b_vm, load_sem.at[2])
    load_s = pltpu.make_async_copy(s_in.at[:, pl.ds(offset, chunk)], s_vm, load_sem.at[3])
    loads = [load_v, load_f, load_b, load_s]
    half = blocks // 2
    gc_loads = []
    for k in range(2):
        rng = pl.ds(k * half, half)
        gc_loads.append(pltpu.make_async_copy(g_in.at[rng], g_vm.at[rng], gc_sem.at[2 * k]))
        gc_loads.append(pltpu.make_async_copy(c_in.at[rng], c_vm.at[rng], gc_sem.at[2 * k + 1]))
    for load in loads + gc_loads:
        load.start()

    barrier = pltpu.get_barrier_semaphore()

    def greet(to_h, to_n):
        pl.semaphore_signal(barrier, inc=1, device_id=(to_h, to_n), device_id_type=MESH)

    for d in range(1, H):
        greet(lax.rem(h + d, H), n)

    @pl.when(n > 0)
    def _():
        for d in range(H):
            greet(lax.rem(h + d, H), n - 1)

    @pl.when(n < N - 1)
    def _():
        for d in range(H):
            greet(lax.rem(h + d, H), n + 1)

    def greeted():
        sides = jnp.where(n > 0, H, 0) + jnp.where(n < N - 1, H, 0)
        pl.semaphore_wait(barrier, H - 1 + sides)

    def remote(src, dst, send, recv, to_h, to_n):
        return pltpu.make_async_remote_copy(
            src_ref=src, dst_ref=dst, send_sem=send, recv_sem=recv,
            device_id=(to_h, to_n), device_id_type=MESH,
        )

    to_high = remote(
        vext.at[blocks], vext.at[0], low_send.at[0], low_recv.at[0], h, lax.rem(n + 1, N)
    )
    to_low = [
        remote(
            vext.at[1], halo.at[h], halo_send.at[d], halo_recv.at[d],
            lax.rem(h + d, H), lax.rem(n + N - 1, N),
        )
        for d in range(H)
    ]
    spills = []
    for i in range(parts):
        to_h = lax.rem(part + i, parts) * dup + twin
        spills.append(
            remote(send_s.at[to_h], recv_s.at[i], s_send.at[i], s_recv.at[i], to_h, lax.rem(n + 1, N))
        )

    load_v.wait()
    for b in range(blocks):
        vext[b + 1] = v_vm[:, b * blk : (b + 1) * blk]
    stacked = halves(v_vm[...])

    to_parts = []
    step = min(256, nodes)
    for i in [*range(1, parts), 0]:
        q = lax.rem(part + i, parts)
        at = pl.multiple_of(q * chunk, 128)
        first = term[0:1, pl.ds(at, chunk)] - n * nodes
        second = term[1:2, pl.ds(at, chunk)] - n * nodes
        first = jnp.where(first == second, -1, first)
        second = jnp.where(first == -1, -1, second)
        piece = jnp.zeros((2 * rows, chunk), f32)
        for k in range(0, nodes, step):
            row = lax.broadcasted_iota(jnp.int32, (step, chunk), 0) + k
            hot = jnp.where(row == first, 1.0, jnp.where(row == second, -1.0, 0.0)).astype(bf16)
            ends[q, k : k + step, :] = hot
            piece += dot(stacked[:, k : k + step], hot)
        piece = piece[:rows] + piece[rows:]
        if i == 0:
            recv_b[h] = piece
        if i or dup > 1:
            send_b[q] = piece
        if i == (1 if parts > 1 else 0):
            greeted()

            @pl.when(n > 0)
            def _():
                for copy in to_low:
                    copy.start()

            @pl.when(n < N - 1)
            def _():
                to_high.start()

        for j in range(dup):
            if i or j:
                to_h = q * dup + lax.rem(twin + j, dup)
                e = i * dup + j
                copy = remote(send_b.at[q], recv_b.at[h], b_send.at[e], b_recv.at[e], to_h, n)
                copy.start()
                to_parts.append(copy)

    @pl.when(n > 0)
    def _():
        to_high.wait_recv()

    @pl.when(n == 0)
    def _():
        vext[0] = jnp.zeros((rows, blk), f32)
        recv_s[...] = jnp.zeros(recv_s.shape, f32)

    @pl.when(n < N - 1)
    def _():
        for copy in to_low:
            copy.wait_recv()

    @pl.when(n == N - 1)
    def _():
        halo[...] = jnp.zeros(halo.shape, f32)

    vext[blocks + 1] = halo[h]

    line = lax.broadcasted_iota(jnp.int32, (rows, blk), 0)
    harmonic = h * (rows // 2) + line // 2
    omega = harmonic.astype(f32) / (H * rows // 2)
    odd = lax.rem(line, 2) == 1

    def linear(r):
        at = [jnp.clip(pat[r, j] - (n * blocks - 1), 0, blocks + 1) for j in range(slots)]
        picks = [vext[at[j]] for j in range(slots)]
        picked = halves(jnp.concatenate(picks, axis=1))
        weight = jnp.concatenate(
            [g_vm[r].reshape(slots * blk, blk), c_vm[r].reshape(slots * blk, blk)], axis=1
        )
        high = weight.astype(bf16)
        low = (weight - high.astype(f32)).astype(bf16)
        main = dot(picked, high)
        rest = dot(picked, low)
        both = main[:rows] + (main[rows:] + rest[:rows])
        conductive, capacitive = both[:, :blk], both[:, blk:]
        turned = jnp.where(
            odd, pltpu.roll(capacitive, 1, 0), -pltpu.roll(capacitive, rows - 1, 0)
        )
        lin[:, r * blk : (r + 1) * blk] = conductive + omega * turned

    for load in gc_loads[:2]:
        load.wait()
    for r in range(half):
        linear(r)

    for copy in to_parts:
        copy.wait_recv()
    first = term[0:1, pl.ds(offset, chunk)] - n * nodes
    second = term[1:2, pl.ds(offset, chunk)] - n * nodes
    row = lax.broadcasted_iota(jnp.int32, (blk, chunk), 0) + nodes
    beyond = jnp.where(row == second, -1.0, 0.0).astype(bf16)
    columns = H * rows
    above = dot(halves(halo[...].reshape(columns, blk)), beyond)
    branch = recv_b[...].reshape(columns, chunk) + (above[:columns] + above[columns:])
    branch_high = branch.astype(bf16)
    branch_low = (branch - branch_high.astype(f32)).astype(bf16)
    load_f.wait()
    load_s.wait()
    wave = dot(f_vm[...], jnp.concatenate([branch_high, branch_low, branch_high], axis=0))
    wave = wave * s_vm[...]
    wave_high = wave.astype(bf16)
    wave_low = (wave - wave_high.astype(f32)).astype(bf16)
    load_b.wait()
    current = dot(b_vm[...], jnp.concatenate([wave_high, wave_low, wave_high], axis=0))
    send_c[...] = current.reshape(H, rows, chunk)
    recv_c[part] = send_c[h]
    to_harm = [None]
    for i in range(1, parts):
        to_h = lax.rem(part + i, parts) * dup + twin
        copy = remote(send_c.at[to_h], recv_c.at[part], c_send.at[i], c_recv.at[i], to_h, n)
        copy.start()
        to_harm.append(copy)
    spill = dot_t(halves(current), beyond)
    send_s[...] = (spill[:columns] + spill[columns:]).reshape(H, rows, blk)

    @pl.when(n < N - 1)
    def _():
        for copy in spills:
            copy.start()

    for load in gc_loads[2:]:
        load.wait()
    for r in range(half, blocks):
        linear(r)

    total = lin[...]
    for i in range(parts):
        q = lax.rem(part + parts - i, parts)
        if i:
            to_harm[i].wait_recv()
        added = dot_t(halves(recv_c[q]), ends[q])
        total = total + (added[:rows] + added[rows:])

    @pl.when(n > 0)
    def _():
        for copy in spills:
            copy.wait_recv()

    arrival = recv_s[0]
    for i in range(1, parts):
        arrival = arrival + recv_s[i]
    out[:, :blk] = total[:, :blk] + arrival
    out[:, blk:] = total[:, blk:]

    for copy in to_parts + to_harm[1:]:
        copy.wait_send()

    @pl.when(n > 0)
    def _():
        for copy in to_low:
            copy.wait_send()

    @pl.when(n < N - 1)
    def _():
        to_high.wait_send()
        for copy in spills:
            copy.wait_send()


def tables(columns, period):
    harmonic = np.arange(columns // 2)
    phases = (np.arange(period)[:, None] * harmonic[None, :]) % period
    angles = phases * (2.0 * math.pi / period)
    forward = np.stack([np.cos(angles), -np.sin(angles)], axis=2).reshape(period, columns)
    backward = forward.T * (2.0 / period)

    def three(table):
        high = table.astype(ml_dtypes.bfloat16)
        low = (table - high.astype(np.float64)).astype(ml_dtypes.bfloat16)
        return jnp.asarray(np.concatenate([high, high, low], axis=1))

    return three(forward), three(backward)


def per_device(voltages, conductance, capacitance, pattern, samples, terminals):
    rows, nodes = voltages.shape
    blocks, slots, blk, _ = conductance.shape
    period, branches = samples.shape
    H, N = lax.axis_size("harm"), lax.axis_size("node")
    parts = min(H, branches // 128)
    dup = H // parts
    chunk = branches // parts
    forward, backward = tables(H * rows, period)
    dma = pltpu.SemaphoreType.DMA
    anywhere = pl.BlockSpec(memory_space=pltpu.MemorySpace.HBM)
    return pl.pallas_call(
        functools.partial(kernel, H, N, parts, dup),
        out_shape=jax.ShapeDtypeStruct((rows, nodes), f32),
        in_specs=[
            pl.BlockSpec(memory_space=pltpu.MemorySpace.SMEM),
            pl.BlockSpec(memory_space=pltpu.MemorySpace.VMEM),
        ]
        + [anywhere] * 6,
        out_specs=pl.BlockSpec(memory_space=pltpu.MemorySpace.VMEM),
        scratch_shapes=[
            pltpu.VMEM((rows, nodes), f32),
            pltpu.VMEM(conductance.shape, f32),
            pltpu.VMEM(capacitance.shape, f32),
            pltpu.VMEM((period, chunk), f32),
            pltpu.VMEM(forward.shape, bf16),
            pltpu.VMEM(backward.shape, bf16),
            pltpu.VMEM((blocks + 2, rows, blk), f32),
            pltpu.VMEM((H, rows, blk), f32),
            pltpu.VMEM((parts, nodes, chunk), bf16),
            pltpu.VMEM((parts, rows, chunk), f32),
            pltpu.VMEM((H, rows, chunk), f32),
            pltpu.VMEM((H, rows, chunk), f32),
            pltpu.VMEM((parts, rows, chunk), f32),
            pltpu.VMEM((H, rows, blk), f32),
            pltpu.VMEM((parts, rows, blk), f32),
            pltpu.VMEM((rows, nodes), f32),
            dma((4,)),
            dma((4,)),
            dma((1,)),
            dma((1,)),
            dma((H,)),
            dma((H,)),
            dma((H,)),
            dma((H,)),
            dma((parts,)),
            dma((parts,)),
            dma((parts,)),
            dma((parts,)),
        ],
        compiler_params=pltpu.CompilerParams(
            collective_id=0, has_side_effects=True, vmem_limit_bytes=40 * 1024 * 1024
        ),
    )(pattern, terminals, voltages, conductance, capacitance, samples, forward, backward)


def solution(mesh):
    in_specs = (
        P("harm", "node"),
        P("node", None, None, None),
        P("node", None, None, None),
        P("node", None),
        P(None, "node"),
        P(None, "node"),
    )
    out_specs = P("harm", "node")
    return jax.shard_map(
        per_device, mesh=mesh, in_specs=in_specs, out_specs=out_specs, check_vma=False
    )
```

time: 139 us -> 24.9 us (0.18); the launches traced: 136 us -> 24.6 us
  other arithmetic: 55.3 us -> 0 us
  local copies, waits for them, and re-layouts: 55.3 us -> 8.9 us
  Pallas kernels: 0 us -> 15.7 us
  blocking collectives: 12.7 us -> 0 us
  starting transfers between devices: 6.2 us -> 0 us
  matrix products: 6.04 us -> 0 us
    gather x5 -> x0, local copies, waits for them, and re-layouts: 41.9 us -> none  [the longest x1 17.3 us: per_device(): diff_coef = jnp.take(spectrum, diff_index, axis=1)]
    add x3 -> x0, other arithmetic: 16.1 us -> none  [the longest x1 15.4 us: per_device(): diff_coef[1] + sum_coef[1]]
    pallas_call x0 -> x1, Pallas kernels: none -> 15.7 us  [per_device(): pl.pallas_call(functools.partial(kernel, H, N, parts, dup), out_shape=jax...]
    select_n x5 -> x0, other arithmetic: 13.9 us -> none  [the longest x2 6.7 us: per_device(): sum_coef = jnp.take(spectrum, sum_index, axis=1)]
    scatter-add x2 -> x0, other arithmetic: 12.9 us -> none  [per_device(): injected.at[:, first_end].add(current).at[:, second_end].add(-current)]
    all_gather x1 -> x0, blocking collectives: 12.7 us -> none  [per_device(): piece = lax.all_gather(padded, 'harm', axis=0, tiled=True)]
    reduce_sum x1 -> x0, other arithmetic: 10.1 us -> none  [per_device(): jnp.sum((diff_coef[0] + sum_coef[0]) * real_in + (sum_coef[1] - diff_coef...]
    ppermute x3 -> x0, starting transfers between devices: 6.2 us -> none  [the longest x1 2.56 us: from_behind(): return lax.ppermute(value, axis, pairs)]
  transfers between devices with their start and end apart: 3 -> 0, of which waited for: 0 -> 0; matrix products, arithmetic and copies ran while one was open for 57% -> 0% of each run, Pallas kernels for 0% -> 0%
where the time goes in v1:
time: 24.9 us; the launch traced here: 24.6 us
  Pallas kernels  15.7 us (63%)
  local copies, waits for them, and re-layouts  8.9 us (36%)
    pallas_call x1, Pallas kernels, per_device(): pl.pallas_call(functools.partial(kernel, H, N, parts, dup), out_shape=jax...  15.7 us
    unnamed x16, local copies, waits for them, and re-layouts  8.9 us

profile of v1, /device:TPU:0, one launch (start us, length us, event | category | flops | bytes accessed | tf_op | source)
XLA Modules:
  0.0 24.6 jit_solution(2006370078906691747)
XLA Ops:
  0.0 0.8 %copy.9.pat = s32[8,3]{1,0:T(8,128)S(1)} copy(s32[8,3]{0,1:T(4,128)} %param.11) | data formatting | bytes 192 | tf_op args[3]
  0.8 0.0 copy-start
  0.8 1.4 %copy-done = f32[8,3,128,128]{3,2,1,0:T(8,128)S(1)} copy-done((f32[8,3,128,128]{3,2,1,0:T(8,128)S(1)}, f32[8,3,128,128]{3,2,1,0:T(8,128)}, u32[]{:S(2)}) %copy-start) | copy-done | bytes 1572888
  2.2 0.0 copy-start.1
  2.2 1.4 %copy-done.1 = f32[8,3,128,128]{3,2,1,0:T(8,128)S(1)} copy-done((f32[8,3,128,128]{3,2,1,0:T(8,128)S(1)}, f32[8,3,128,128]{3,2,1,0:T(8,128)}, u32[]{:S(2)}) %copy-start.1) | copy-done | bytes 1572888
  3.6 0.0 copy-start.2
  3.6 1.2 %copy-done.2 = f32[256,1024]{1,0:T(8,128)S(1)} copy-done((f32[256,1024]{1,0:T(8,128)S(1)}, f32[256,1024]{1,0:T(8,128)}, u32[]{:S(2)}) %copy-start.2) | copy-done | bytes 1048600
  4.8 0.0 copy-start.3
  4.8 0.9 %copy-done.3 = bf16[128,768]{1,0:T(8,128)(2,1)S(1)} copy-done((bf16[128,768]{1,0:T(8,128)(2,1)S(1)}, bf16[128,768]{1,0:T(8,128)(2,1)}, u32[]{:S(2)}) %copy-start.3) | copy-done | bytes 196632
  5.7 0.0 copy-start.4
  5.7 0.9 %copy-done.4 = bf16[256,384]{1,0:T(8,128)(2,1)S(1)} copy-done((bf16[256,384]{1,0:T(8,128)(2,1)S(1)}, bf16[256,384]{1,0:T(8,128)(2,1)}, u32[]{:S(2)}) %copy-start.4) | copy-done | bytes 196632
  6.7 0.0 copy-start.5
  6.7 0.9 %copy-done.5 = f32[32,1024]{1,0:T(8,128)S(1)} copy-done((f32[32,1024]{1,0:T(8,128)S(1)}, f32[32,1024]{1,0:T(8,128)}, u32[]{:S(2)}) %copy-start.5) | copy-done | bytes 131096
  7.6 0.0 copy-start.6
  7.6 0.7 %copy-done.6 = s32[2,1024]{1,0:T(2,128)S(1)} copy-done((s32[2,1024]{1,0:T(2,128)S(1)}, s32[2,1024]{1,0:T(2,128)}, u32[]{:S(2)}) %copy-start.6) | copy-done | bytes 8216
  8.3 15.7 %shard_map.82 = f32[32,1024]{1,0:T(8,128)S(1)} custom-call(s32[8,3]{1,0:T(8,128)S(1)} %copy.9.pat, s32[2,1024]{1,0:T(2,128)S(1)} %copy-done.6, f32[32,1024]{1,0:T(8,128)S(1)} %copy-done.5, f32[8,3,128,128]{3,2,1,0:T(8,128)S(1)} %copy-done, f32[8,3,128,128]{3,2,1,0:T(8,128)S(1)} %copy-done.1, f32[256,1024]{1,0:T(8,128)S(1)} %copy-done.2, ...), custom_call_target="tpu_custom_call" | custom-call | tf_op jit(solution)/shard_map/pallas_call | solution.py:299
  23.9 0.7 %copy.11 = f32[32,1024]{1,0:T(8,128)} copy(f32[32,1024]{1,0:T(8,128)S(1)} %shard_map.82) | data formatting | bytes 262144
Async XLA Ops:
  0.8 1.4 %copy-start = (f32[8,3,128,128]{3,2,1,0:T(8,128)S(1)}, f32[8,3,128,128]{3,2,1,0:T(8,128)}, u32[]{:S(2)}) copy-start(f32[8,3,128,128]{3,2,1,0:T(8,128)} %g_in.1) | copy-start | bytes 4718596
  2.2 1.4 %copy-start.1 = (f32[8,3,128,128]{3,2,1,0:T(8,128)S(1)}, f32[8,3,128,128]{3,2,1,0:T(8,128)}, u32[]{:S(2)}) copy-start(f32[8,3,128,128]{3,2,1,0:T(8,128)} %c_in.1) | copy-start | bytes 4718596
  3.6 1.2 %copy-start.2 = (f32[256,1024]{1,0:T(8,128)S(1)}, f32[256,1024]{1,0:T(8,128)}, u32[]{:S(2)}) copy-start(f32[256,1024]{1,0:T(8,128)} %s_in.1) | copy-start | bytes 3145732
  4.8 0.9 %copy-start.3 = (bf16[128,768]{1,0:T(8,128)(2,1)S(1)}, bf16[128,768]{1,0:T(8,128)(2,1)}, u32[]{:S(2)}) copy-start(bf16[128,768]{1,0:T(8,128)(2,1)} %constant.5.clone.b_in) | copy-start | bytes 589828
  5.7 0.9 %copy-start.4 = (bf16[256,384]{1,0:T(8,128)(2,1)S(1)}, bf16[256,384]{1,0:T(8,128)(2,1)}, u32[]{:S(2)}) copy-start(bf16[256,384]{1,0:T(8,128)(2,1)} %constant.4.clone.f_in) | copy-start | bytes 589828
  6.7 0.9 %copy-start.5 = (f32[32,1024]{1,0:T(8,128)S(1)}, f32[32,1024]{1,0:T(8,128)}, u32[]{:S(2)}) copy-start(f32[32,1024]{1,0:T(8,128)} %v_in.1) | copy-start | bytes 393220
  7.6 0.7 %copy-start.6 = (s32[2,1024]{1,0:T(2,128)S(1)}, s32[2,1024]{1,0:T(2,128)}, u32[]{:S(2)}) copy-start(s32[2,1024]{1,0:T(2,128)} %term.1) | copy-start | bytes 24580

commit v2 on v1

--- a/solution.py
+++ b/solution.py
@@ -174,7 +174,7 @@
     odd = lax.rem(line, 2) == 1
 
     def linear(r):
-        at = [jnp.clip(pat[r, j] - (n * blocks - 1), 0, blocks + 1) for j in range(slots)]
+        at = [jnp.clip(pat[j, r] - (n * blocks - 1), 0, blocks + 1) for j in range(slots)]
         picks = [vext[at[j]] for j in range(slots)]
         picked = halves(jnp.concatenate(picks, axis=1))
         weight = jnp.concatenate(
@@ -336,9 +336,9 @@
             dma((parts,)),
         ],
         compiler_params=pltpu.CompilerParams(
-            collective_id=0, has_side_effects=True, vmem_limit_bytes=40 * 1024 * 1024
+            collective_id=0, has_side_effects=True, vmem_limit_bytes=63 * 1024 * 1024
         ),
-    )(pattern, terminals, voltages, conductance, capacitance, samples, forward, backward)
+    )(pattern.T, terminals, voltages, conductance, capacitance, samples, forward, backward)
 
 
 def solution(mesh):

time: 24.9 us -> 17.3 us (0.69)
  local copies, waits for them, and re-layouts: 8.9 us -> 1.57 us
    unnamed x16 -> x1, local copies, waits for them, and re-layouts: 8.9 us -> 1.57 us
where the time goes in v2:
time: 17.3 us; the launch traced here: 17.1 us
  Pallas kernels  15.5 us (90%)
  local copies, waits for them, and re-layouts  1.57 us (9%)
    pallas_call x1, Pallas kernels, per_device(): pl.pallas_call(functools.partial(kernel, H, N, parts, dup), out_shape=jax...  15.5 us
    unnamed x1, local copies, waits for them, and re-layouts  1.57 us

profile of v2, /device:TPU:0, one launch (start us, length us, event | category | flops | bytes accessed | tf_op | source)
XLA Modules:
  0.0 17.1 jit_solution(16447798903863393772)
XLA Ops:
  0.0 15.5 %shard_map.82 = f32[32,1024]{1,0:T(8,128)} custom-call(s32[3,8]{1,0:T(4,128)} %bitcast.1, s32[2,1024]{1,0:T(2,128)} %term.1, f32[32,1024]{1,0:T(8,128)} %v_in.1, f32[8,3,128,128]{3,2,1,0:T(8,128)} %g_in.1, f32[8,3,128,128]{3,2,1,0:T(8,128)} %c_in.1, f32[256,1024]{1,0:T(8,128)} %s_in.1, bf16[256,384]{1,0:T(8,128)(2,1)} %constant.4.clone.f_in, ...), custom_call_target="tpu_custom_call" | custom-call | tf_op jit(solution)/shard_map/pallas_call | solution.py:299
  15.5 1.6 %copy.10 = f32[32,1024]{1,0:T(8,128)} copy(f32[32,1024]{1,0:T(8,128)} %shard_map.82) | data formatting | bytes 262144

commit v3 on v2

--- a/solution.py
+++ b/solution.py
@@ -29,9 +29,9 @@
 
 def kernel(
     H, N, parts, dup,
-    pat, term, v_in, g_in, c_in, s_in, f_in, b_in,
+    pat_in, term_in, v_in, g_in, c_in, s_in, f_in, b_in,
     out,
-    v_vm, g_vm, c_vm, s_vm, f_vm, b_vm,
+    pat, term, v_vm, g_vm, c_vm, s_vm, f_vm, b_vm,
     vext, halo, ends, send_b, recv_b, send_c, recv_c, send_s, recv_s, lin,
     load_sem, gc_sem,
     low_send, low_recv, halo_send, halo_recv,
@@ -44,11 +44,31 @@
     part, twin = h // dup, lax.rem(h, dup)
     offset = pl.multiple_of(part * chunk, 128)
 
+    barrier = pltpu.get_barrier_semaphore()
+
+    def greet(to_h, to_n):
+        pl.semaphore_signal(barrier, inc=1, device_id=(to_h, to_n), device_id_type=MESH)
+
+    for d in range(1, H):
+        greet(lax.rem(h + d, H), n)
+
+    @pl.when(n > 0)
+    def _():
+        for d in range(H):
+            greet(lax.rem(h + d, H), n - 1)
+
+    @pl.when(n < N - 1)
+    def _():
+        for d in range(H):
+            greet(lax.rem(h + d, H), n + 1)
+
     load_v = pltpu.make_async_copy(v_in, v_vm, load_sem.at[0])
     load_f = pltpu.make_async_copy(f_in, f_vm, load_sem.at[1])
     load_b = pltpu.make_async_copy(b_in, b_vm, load_sem.at[2])
     load_s = pltpu.make_async_copy(s_in.at[:, pl.ds(offset, chunk)], s_vm, load_sem.at[3])
-    loads = [load_v, load_f, load_b, load_s]
+    load_t = pltpu.make_async_copy(term_in, term, load_sem.at[4])
+    load_p = pltpu.make_async_copy(pat_in, pat, load_sem.at[5])
+    loads = [load_v, load_t, load_p, load_f, load_b, load_s]
     half = blocks // 2
     gc_loads = []
     for k in range(2):
@@ -58,24 +78,6 @@
     for load in loads + gc_loads:
         load.start()
 
-    barrier = pltpu.get_barrier_semaphore()
-
-    def greet(to_h, to_n):
-        pl.semaphore_signal(barrier, inc=1, device_id=(to_h, to_n), device_id_type=MESH)
-
-    for d in range(1, H):
-        greet(lax.rem(h + d, H), n)
-
-    @pl.when(n > 0)
-    def _():
-        for d in range(H):
-            greet(lax.rem(h + d, H), n - 1)
-
-    @pl.when(n < N - 1)
-    def _():
-        for d in range(H):
-            greet(lax.rem(h + d, H), n + 1)
-
     def greeted():
         sides = jnp.where(n > 0, H, 0) + jnp.where(n < N - 1, H, 0)
         pl.semaphore_wait(barrier, H - 1 + sides)
@@ -103,6 +105,7 @@
             remote(send_s.at[to_h], recv_s.at[i], s_send.at[i], s_recv.at[i], to_h, lax.rem(n + 1, N))
         )
 
+    load_t.wait()
     load_v.wait()
     for b in range(blocks):
         vext[b + 1] = v_vm[:, b * blk : (b + 1) * blk]
@@ -191,6 +194,7 @@
         )
         lin[:, r * blk : (r + 1) * blk] = conductive + omega * turned
 
+    load_p.wait()
     for load in gc_loads[:2]:
         load.wait()
     for r in range(half):
@@ -298,14 +302,12 @@
     anywhere = pl.BlockSpec(memory_space=pltpu.MemorySpace.HBM)
     return pl.pallas_call(
         functools.partial(kernel, H, N, parts, dup),
-        out_shape=jax.ShapeDtypeStruct((rows, nodes), f32),
-        in_specs=[
-            pl.BlockSpec(memory_space=pltpu.MemorySpace.SMEM),
-            pl.BlockSpec(memory_space=pltpu.MemorySpace.VMEM),
-        ]
-        + [anywhere] * 6,
+        out_shape=pltpu.VMEM((rows, nodes), f32),
+        in_specs=[anywhere] * 8,
         out_specs=pl.BlockSpec(memory_space=pltpu.MemorySpace.VMEM),
         scratch_shapes=[
+            pltpu.SMEM(pattern.shape[::-1], jnp.int32),
+            pltpu.VMEM(terminals.shape, jnp.int32),
             pltpu.VMEM((rows, nodes), f32),
             pltpu.VMEM(conductance.shape, f32),
             pltpu.VMEM(capacitance.shape, f32),
@@ -322,7 +324,7 @@
             pltpu.VMEM((H, rows, blk), f32),
             pltpu.VMEM((parts, rows, blk), f32),
             pltpu.VMEM((rows, nodes), f32),
-            dma((4,)),
+            dma((6,)),
             dma((4,)),
             dma((1,)),
             dma((1,)),

time: 17.3 us -> 15 us (0.87)
  Pallas kernels: 15.5 us -> 14.2 us
  local copies, waits for them, and re-layouts: 1.57 us -> 0.66 us
    pallas_call x1, Pallas kernels: 15.5 us -> 14.2 us  [per_device(): pl.pallas_call(functools.partial(kernel, H, N, parts, dup), out_shape=plt...]
    unnamed x1, local copies, waits for them, and re-layouts: 1.57 us -> 0.66 us
where the time goes in v3:
time: 15 us; the launch traced here: 14.8 us
  Pallas kernels  14.2 us (95%)
  local copies, waits for them, and re-layouts  0.66 us (4%)
    pallas_call x1, Pallas kernels, per_device(): pl.pallas_call(functools.partial(kernel, H, N, parts, dup), out_shape=plt...  14.2 us
    unnamed x1, local copies, waits for them, and re-layouts  0.66 us

profile of v3, /device:TPU:0, one launch (start us, length us, event | category | flops | bytes accessed | tf_op | source)
XLA Modules:
  0.0 14.8 jit_solution(13261166664573569792)
XLA Ops:
  0.0 14.2 %shard_map.82 = f32[32,1024]{1,0:T(8,128)S(1)} custom-call(s32[3,8]{1,0:T(4,128)} %bitcast.1, s32[2,1024]{1,0:T(2,128)} %term_in.1, f32[32,1024]{1,0:T(8,128)} %v_in.1, f32[8,3,128,128]{3,2,1,0:T(8,128)} %g_in.1, f32[8,3,128,128]{3,2,1,0:T(8,128)} %c_in.1, f32[256,1024]{1,0:T(8,128)} %s_in.1, bf16[256,384]{1,0:T(8,128)(2,1)} %constant.4.clone.f_in, ...), custom_call_target="tpu_custom_call" | custom-call | tf_op jit(solution)/shard_map/pallas_call | solution.py:303
  14.2 0.7 %copy.10 = f32[32,1024]{1,0:T(8,128)} copy(f32[32,1024]{1,0:T(8,128)S(1)} %shard_map.82) | data formatting | bytes 262144

commit v4 on v3

--- a/solution.py
+++ b/solution.py
@@ -124,7 +124,6 @@
         for k in range(0, nodes, step):
             row = lax.broadcasted_iota(jnp.int32, (step, chunk), 0) + k
             hot = jnp.where(row == first, 1.0, jnp.where(row == second, -1.0, 0.0)).astype(bf16)
-            ends[q, k : k + step, :] = hot
             piece += dot(stacked[:, k : k + step], hot)
         piece = piece[:rows] + piece[rows:]
         if i == 0:
@@ -151,6 +150,19 @@
                 copy.start()
                 to_parts.append(copy)
 
+    lane = lax.broadcasted_iota(jnp.int32, (chunk, blk), 1)
+    for q in range(parts):
+        first = term[0:1, q * chunk : (q + 1) * chunk] - n * nodes
+        second = term[1:2, q * chunk : (q + 1) * chunk] - n * nodes
+        first = jnp.where(first == second, -1, first)
+        second = jnp.where(first == -1, -1, second)
+        first = jnp.broadcast_to(first, (blk, chunk)).T
+        second = jnp.broadcast_to(second, (blk, chunk)).T
+        for k in range(0, nodes, blk):
+            node = lane + k
+            hot = jnp.where(node == first, 1.0, jnp.where(node == second, -1.0, 0.0))
+            ends[q, :, k : k + blk] = hot.astype(bf16)
+
     @pl.when(n > 0)
     def _():
         to_high.wait_recv()
@@ -195,10 +207,6 @@
         lin[:, r * blk : (r + 1) * blk] = conductive + omega * turned
 
     load_p.wait()
-    for load in gc_loads[:2]:
-        load.wait()
-    for r in range(half):
-        linear(r)
 
     for copy in to_parts:
         copy.wait_recv()
@@ -235,9 +243,9 @@
         for copy in spills:
             copy.start()
 
-    for load in gc_loads[2:]:
+    for load in gc_loads:
         load.wait()
-    for r in range(half, blocks):
+    for r in range(blocks):
         linear(r)
 
     total = lin[...]
@@ -245,7 +253,7 @@
         q = lax.rem(part + parts - i, parts)
         if i:
             to_harm[i].wait_recv()
-        added = dot_t(halves(recv_c[q]), ends[q])
+        added = dot(halves(recv_c[q]), ends[q])
         total = total + (added[:rows] + added[rows:])
 
     @pl.when(n > 0)
@@ -316,7 +324,7 @@
             pltpu.VMEM(backward.shape, bf16),
             pltpu.VMEM((blocks + 2, rows, blk), f32),
             pltpu.VMEM((H, rows, blk), f32),
-            pltpu.VMEM((parts, nodes, chunk), bf16),
+            pltpu.VMEM((parts, chunk, nodes), bf16),
             pltpu.VMEM((parts, rows, chunk), f32),
             pltpu.VMEM((H, rows, chunk), f32),
             pltpu.VMEM((H, rows, chunk), f32),

time: 15 us -> 14.7 us (0.980)
  Pallas kernels: 14.2 us -> 13.9 us
    pallas_call x1, Pallas kernels: 14.2 us -> 13.9 us  [per_device(): pl.pallas_call(functools.partial(kernel, H, N, parts, dup), out_shape=plt...]
where the time goes in v4:
time: 14.7 us; the launch traced here: 14.6 us
  Pallas kernels  13.9 us (95%)
  local copies, waits for them, and re-layouts  0.66 us (4%)
    pallas_call x1, Pallas kernels, per_device(): pl.pallas_call(functools.partial(kernel, H, N, parts, dup), out_shape=plt...  13.9 us
    unnamed x1, local copies, waits for them, and re-layouts  0.66 us

profile of v4, /device:TPU:0, one launch (start us, length us, event | category | flops | bytes accessed | tf_op | source)
XLA Modules:
  0.0 14.6 jit_solution(11321752751243106053)
XLA Ops:
  0.0 13.9 %shard_map.82 = f32[32,1024]{1,0:T(8,128)S(1)} custom-call(s32[3,8]{1,0:T(4,128)} %bitcast.1, s32[2,1024]{1,0:T(2,128)} %term_in.1, f32[32,1024]{1,0:T(8,128)} %v_in.1, f32[8,3,128,128]{3,2,1,0:T(8,128)} %g_in.1, f32[8,3,128,128]{3,2,1,0:T(8,128)} %c_in.1, f32[256,1024]{1,0:T(8,128)} %s_in.1, bf16[256,384]{1,0:T(8,128)(2,1)} %constant.4.clone.f_in, ...), custom_call_target="tpu_custom_call" | custom-call | tf_op jit(solution)/shard_map/pallas_call | solution.py:311
  13.9 0.7 %copy.10 = f32[32,1024]{1,0:T(8,128)} copy(f32[32,1024]{1,0:T(8,128)S(1)} %shard_map.82) | data formatting | bytes 262144

commit v5 on v4

--- a/solution.py
+++ b/solution.py
@@ -21,10 +21,6 @@
 
 def dot(a, b):
     return jnp.dot(a, b, preferred_element_type=f32)
-
-
-def dot_t(a, b):
-    return lax.dot_general(a, b, (((1,), (1,)), ((), ())), preferred_element_type=f32)
 
 
 def kernel(
@@ -208,24 +204,28 @@
 
     load_p.wait()
 
-    for copy in to_parts:
-        copy.wait_recv()
     first = term[0:1, pl.ds(offset, chunk)] - n * nodes
     second = term[1:2, pl.ds(offset, chunk)] - n * nodes
     row = lax.broadcasted_iota(jnp.int32, (blk, chunk), 0) + nodes
     beyond = jnp.where(row == second, -1.0, 0.0).astype(bf16)
     columns = H * rows
     above = dot(halves(halo[...].reshape(columns, blk)), beyond)
-    branch = recv_b[...].reshape(columns, chunk) + (above[:columns] + above[columns:])
+    above = above[:columns] + above[columns:]
+    node = lax.broadcasted_iota(jnp.int32, (chunk, blk), 1) + nodes
+    second = jnp.broadcast_to(second, (blk, chunk)).T
+    beyond_back = jnp.where(node == second, -1.0, 0.0).astype(bf16)
+    load_f.wait()
+    load_s.wait()
+    load_b.wait()
+    for copy in to_parts:
+        copy.wait_recv()
+    branch = recv_b[...].reshape(columns, chunk) + above
     branch_high = branch.astype(bf16)
     branch_low = (branch - branch_high.astype(f32)).astype(bf16)
-    load_f.wait()
-    load_s.wait()
     wave = dot(f_vm[...], jnp.concatenate([branch_high, branch_low, branch_high], axis=0))
     wave = wave * s_vm[...]
     wave_high = wave.astype(bf16)
     wave_low = (wave - wave_high.astype(f32)).astype(bf16)
-    load_b.wait()
     current = dot(b_vm[...], jnp.concatenate([wave_high, wave_low, wave_high], axis=0))
     send_c[...] = current.reshape(H, rows, chunk)
     recv_c[part] = send_c[h]
@@ -235,7 +235,7 @@
         copy = remote(send_c.at[to_h], recv_c.at[part], c_send.at[i], c_recv.at[i], to_h, n)
         copy.start()
         to_harm.append(copy)
-    spill = dot_t(halves(current), beyond)
+    spill = dot(halves(current), beyond_back)
     send_s[...] = (spill[:columns] + spill[columns:]).reshape(H, rows, blk)
 
     @pl.when(n < N - 1)

time: 14.7 us -> 14.5 us (0.986)
  Pallas kernels: 13.9 us -> 13.7 us
    pallas_call x1, Pallas kernels: 13.9 us -> 13.7 us  [per_device(): pl.pallas_call(functools.partial(kernel, H, N, parts, dup), out_shape=plt...]
where the time goes in v5:
time: 14.5 us; the launch traced here: 14.3 us
  Pallas kernels  13.7 us (94%)
  local copies, waits for them, and re-layouts  0.66 us (5%)
    pallas_call x1, Pallas kernels, per_device(): pl.pallas_call(functools.partial(kernel, H, N, parts, dup), out_shape=plt...  13.7 us
    unnamed x1, local copies, waits for them, and re-layouts  0.66 us

profile of v5, /device:TPU:0, one launch (start us, length us, event | category | flops | bytes accessed | tf_op | source)
XLA Modules:
  0.0 14.3 jit_solution(13110848570588370210)
XLA Ops:
  0.0 13.7 %shard_map.82 = f32[32,1024]{1,0:T(8,128)S(1)} custom-call(s32[3,8]{1,0:T(4,128)} %bitcast.1, s32[2,1024]{1,0:T(2,128)} %term_in.1, f32[32,1024]{1,0:T(8,128)} %v_in.1, f32[8,3,128,128]{3,2,1,0:T(8,128)} %g_in.1, f32[8,3,128,128]{3,2,1,0:T(8,128)} %c_in.1, f32[256,1024]{1,0:T(8,128)} %s_in.1, bf16[256,384]{1,0:T(8,128)(2,1)} %constant.4.clone.f_in, ...), custom_call_target="tpu_custom_call" | custom-call | tf_op jit(solution)/shard_map/pallas_call | solution.py:311
  13.7 0.7 %copy.10 = f32[32,1024]{1,0:T(8,128)} copy(f32[32,1024]{1,0:T(8,128)S(1)} %shard_map.82) | data formatting | bytes 262144

commit v6 on v5

--- a/solution.py
+++ b/solution.py
@@ -71,7 +71,7 @@
         rng = pl.ds(k * half, half)
         gc_loads.append(pltpu.make_async_copy(g_in.at[rng], g_vm.at[rng], gc_sem.at[2 * k]))
         gc_loads.append(pltpu.make_async_copy(c_in.at[rng], c_vm.at[rng], gc_sem.at[2 * k + 1]))
-    for load in loads + gc_loads:
+    for load in loads:
         load.start()
 
     def greeted():
@@ -103,6 +103,8 @@
 
     load_t.wait()
     load_v.wait()
+    for load in gc_loads:
+        load.start()
     for b in range(blocks):
         vext[b + 1] = v_vm[:, b * blk : (b + 1) * blk]
     stacked = halves(v_vm[...])

time: 14.5 us -> 14.5 us (level)
  no operation moved by 1% of the time
where the time goes in v6:
time: 14.5 us; the launch traced here: 14.3 us
  Pallas kernels  13.7 us (94%)
  local copies, waits for them, and re-layouts  0.66 us (5%)
    pallas_call x1, Pallas kernels, per_device(): pl.pallas_call(functools.partial(kernel, H, N, parts, dup), out_shape=plt...  13.7 us
    unnamed x1, local copies, waits for them, and re-layouts  0.66 us

profile of v6, /device:TPU:0, one launch (start us, length us, event | category | flops | bytes accessed | tf_op | source)
XLA Modules:
  0.0 14.3 jit_solution(16826465101477934749)
XLA Ops:
  0.0 13.7 %shard_map.82 = f32[32,1024]{1,0:T(8,128)S(1)} custom-call(s32[3,8]{1,0:T(4,128)} %bitcast.1, s32[2,1024]{1,0:T(2,128)} %term_in.1, f32[32,1024]{1,0:T(8,128)} %v_in.1, f32[8,3,128,128]{3,2,1,0:T(8,128)} %g_in.1, f32[8,3,128,128]{3,2,1,0:T(8,128)} %c_in.1, f32[256,1024]{1,0:T(8,128)} %s_in.1, bf16[256,384]{1,0:T(8,128)(2,1)} %constant.4.clone.f_in, ...), custom_call_target="tpu_custom_call" | custom-call | tf_op jit(solution)/shard_map/pallas_call | solution.py:313
  13.7 0.7 %copy.10 = f32[32,1024]{1,0:T(8,128)} copy(f32[32,1024]{1,0:T(8,128)S(1)} %shard_map.82) | data formatting | bytes 262144
